TPU v7x, 32 devices: a whole 2x2x4 slice. The times are simulated.
32 devices in a mesh: node: 16 (over z, y, x), local: 2 (over core).
Axes of the slice: x: 2, y: 2, z: 4, core: 2. Of those that a mesh axis runs over, the one named last changes fastest.
Arguments:
- grad_out: bfloat16 [2048, 7168], P('node', 'local'), may hold values from -6 to 6
- probs: bfloat16 [2048, 8], P('node'), may hold values from 0.099609375 to 2.5
- node_list: int32 [2048, 4], P('node'), may hold values from 0 to 15, all different within a row; in each aligned block of 128 rows (0 to 127, 128 to 255, ...) at most 48 rows name the same one
- weight_down: bfloat16 [32, 1024, 7168], P('node', 'local'), may hold values from -0.1875 to 0.1875
- saved_hidden: bfloat16 [32, 768, 1024], P('node', None, 'local'), may hold values from -0.1875 to 0.1875
Outputs:
- grad_hidden: bfloat16 [32, 768, 1024], P('node', None, 'local')
- grad_probs: float32 [2048, 8], P('node')
Inputs may be any that keep to these rules, and one draw needn't show every extreme that they name: `node_list`: each token lists 4 different nodes. Among the 128 tokens of one index of node, at most 48 list any one node, and some node is listed by exactly 48 of them.
All inputs are finite; a program needn't handle non-finite values.
Results may differ from a plain program's by a relative error of at most 0.001.
Values may be sent and summed in bfloat16 or wider, within the bound.
A program may use at most 128 MiB of HBM per device.

v0:
```python
import jax
import jax.numpy as jnp
from jax import lax
from jax.sharding import PartitionSpec as P


def gather_slots(source, source_row, slot_valid):
    padded = jnp.concatenate([source, jnp.zeros((1, source.shape[1]), source.dtype)], axis=0)
    index = jnp.where(slot_valid, source_row, source.shape[0])
    return jnp.take(padded, index, axis=0)


def on_device(grad_out, probs, node_list, weight_down, saved_hidden):
    node_count = lax.axis_size("node")
    tok_rows = node_list.shape[0]
    route_count = node_list.shape[1]
    slot_rows = saved_hidden.shape[1]
    capacity = slot_rows // node_count
    expert_count = weight_down.shape[0]
    node_ids = lax.broadcasted_iota(jnp.int32, (tok_rows, route_count, node_count), 2)
    listed = (node_list[:, :, None] == node_ids).astype(jnp.float32)
    member = jnp.sum((node_list[:, :, None] == node_ids).astype(jnp.int32), axis=1)
    arrival = jnp.cumsum(member, axis=0) - member
    positions = lax.broadcasted_iota(jnp.int32, (tok_rows, node_count, capacity), 2)
    select_mask = (arrival[:, :, None] == positions) & (member[:, :, None] == 1)
    select_count = select_mask.astype(jnp.int32)
    token_iota = lax.broadcasted_iota(jnp.int32, (tok_rows, node_count, capacity), 0)
    source_row = jnp.sum(select_count * token_iota, axis=0)
    slot_valid = jnp.sum(select_count, axis=0) > 0
    select_full = select_mask.astype(jnp.float32)
    grouped = probs.reshape(tok_rows, route_count, expert_count).astype(jnp.float32)
    picked = jnp.einsum("tjm,tjc->tmc", listed, grouped, precision=lax.Precision.HIGHEST)
    prob_send = jnp.einsum(
        "tms,tmc->msc", select_full, picked, precision=lax.Precision.HIGHEST
    ).astype(jnp.bfloat16)
    full_rows = lax.all_gather(grad_out, "local", axis=1, tiled=True)
    rows_send = gather_slots(full_rows, source_row, slot_valid)
    rows_in, prob_in = (
        lax.all_to_all(rows_send, "node", split_axis=0, concat_axis=0, tiled=True),
        lax.all_to_all(prob_send, "node", split_axis=0, concat_axis=0, tiled=True),
    )
    hidden_grads = jnp.einsum(
        "rd,ehd->erh",
        rows_in.reshape(slot_rows, -1),
        weight_down,
        preferred_element_type=jnp.float32,
    )
    scales = jnp.transpose(prob_in.reshape(slot_rows, expert_count).astype(jnp.float32))
    grad_hidden = (scales[:, :, None] * hidden_grads).astype(jnp.bfloat16)
    partial_value = jnp.sum(saved_hidden.astype(jnp.float32) * hidden_grads, axis=2)
    partial_value = jnp.transpose(partial_value).reshape(node_count, capacity, expert_count)
    summed = lax.psum(partial_value, "local")
    returned = lax.all_to_all(summed, "node", split_axis=0, concat_axis=0, tiled=True)
    per_node = jnp.einsum("tms,msc->tmc", select_full, returned, precision=lax.Precision.HIGHEST)
    grad_probs = jnp.einsum("tjm,tmc->tjc", listed, per_node, precision=lax.Precision.HIGHEST)
    return (grad_hidden, grad_probs.reshape(tok_rows, route_count * expert_count))


def solution(mesh):
    return jax.shard_map(
        on_device,
        mesh=mesh,
        in_specs=(
            P("node", "local"),
            P("node", None),
            P("node", None),
            P("node", "local", None),
            P("node", None, "local"),
        ),
        out_specs=(P("node", None, "local"), P("node", None)),
        check_vma=False,
    )
```

profile of v0, /device:TPU:0, one launch (start us, length us, event | category | flops | bytes accessed | tf_op | source)
XLA Modules:
  0.0 345.5 jit_solution(12832174122178947112)
XLA Ops:
  7.2 0.0 all-gather.2.cloned.1.call-start
  7.2 0.7 all-gather.2.cloned.1.call-update
  7.9 0.8 copy.51
  8.7 0.3 convert_reduce_fusion.1
  9.0 0.1 copy.53
  9.0 0.2 reduce_window_sum.11
  9.2 0.1 copy.52
  9.3 0.8 copy.54
  10.1 0.3 fusion.6
  10.4 0.1 copy.55
  10.5 1.0 convolution_convert_fusion
  11.6 8.3 %all-to-all-start = ((bf16[16,48,2]{1,2,0:T(2,128)(2,1)}), bf16[16,48,2]{1,2,0:T(2,128)(2,1)S(1)}, u32[]{:S(2)}, u32[]{:S(2)}) async-start(bf16[16,48,2]{1,2,0:T(2,128)(2,1)} %convolution_convert_fusion), calls=%async_computation | async-start | bytes 16384 | tf_op jit(solution)/shard_map/all_to_all | solution.py:40
  19.9 0.6 convert_reduce_fusion
  20.5 0.1 reshape.74
  20.6 1.8 all-gather.2.cloned.1.call-done
  22.5 1.7 concatenate.3
  24.2 9.4 %gather_fusion = bf16[768,7168]{1,0:T(8,128)(2,1)} fusion(bf16[129,7168]{1,0:T(8,128)(2,1)S(1)} %concatenate.3, s32[1024]{0:T(1024)S(1)} %pad_clamp_fusion), kind=kCustom, calls=%fused_computation | custom fusion | bytes 22023168 | tf_op jit(solution)/shard_map/jit(_take)/gather | solution.py:10
  33.6 9.9 %broadcast_select_fusion = bf16[16,48,7168]{2,1,0:T(8,128)(2,1)} fusion(bf16[16,48,7168]{2,1,0:T(8,128)(2,1)} %bitcast.31, pred[16,48]{1,0:T(8,128)(4,1)S(1)} %compare_and_fusion), kind=kLoop, calls=%fused_computation.1 | loop fusion | flops 5505024 | bytes 22020864 | tf_op jit(solution)/shard_map/jit(_take)/select_n | solution.py:10
  43.4 0.0 copy-start
  43.4 0.0 all-to-all-done
  43.4 7.0 %all-to-all-start.1 = ((bf16[16,48,7168]{2,1,0:T(8,128)(2,1)}), bf16[16,48,7168]{2,1,0:T(8,128)(2,1)}, u32[]{:S(2)}, u32[]{:S(2)}) async-start(bf16[16,48,7168]{2,1,0:T(8,128)(2,1)} %broadcast_select_fusion), calls=%async_computation.1 | async-start | bytes 22020096 | tf_op jit(solution)/shard_map/all_to_all | solution.py:39
  50.4 0.0 copy-done
  50.4 0.7 copy.57
  51.1 0.1 reshape.71
  51.2 207.7 %all-to-all-done.1 = bf16[16,48,7168]{2,1,0:T(8,128)(2,1)} async-done(((bf16[16,48,7168]{2,1,0:T(8,128)(2,1)}), bf16[16,48,7168]{2,1,0:T(8,128)(2,1)}, u32[]{:S(2)}, u32[]{:S(2)}) %all-to-all-start.1) | async-done | bytes 11010080 | tf_op jit(solution)/shard_map/all_to_all | solution.py:39
  258.9 18.1 %fusion.1 = (f32[2,768]{1,0:T(2,128)S(1)}, bf16[2,768,512]{1,2,0:T(8,128)(2,1)S(1)}) fusion(bf16[2,768,512]{1,2,0:T(8,128)(2,1)S(1)} %copy.57, f32[2,768]{1,0:T(2,128)S(1)} %bitcast.32, bf16[768,7168,1]{1,0,2:T(8,128)(2,1)} %bitcast.5, bf16[2,512,7168]{2,1,0:T(8,128)(2,1)} %param.8), kind=kOutput, calls=%fused_computation.5 | convolution fusion | flops 11278219264 | bytes 28848128 | tf_op jit(solution)/shard_map/rd,ehd->erh/dot_general | solution.py:42
  277.0 0.1 reshape.69
  277.1 3.4 psum.7
  280.5 0.6 copy.58
  281.1 48.5 %all-to-all-start.2 = ((f32[16,48,2]{1,2,0:T(2,128)}), f32[16,48,2]{1,2,0:T(2,128)S(1)}, u32[]{:S(2)}, u32[]{:S(2)}) async-start(f32[16,48,2]{1,2,0:T(2,128)} %copy.58), calls=%async_computation.2 | async-start | bytes 32768 | tf_op jit(solution)/shard_map/all_to_all | solution.py:53
  329.5 1.6 copy.61
  331.1 5.8 %all-to-all-done.2 = f32[16,48,2]{1,2,0:T(2,128)S(1)} async-done(((f32[16,48,2]{1,2,0:T(2,128)}), f32[16,48,2]{1,2,0:T(2,128)S(1)}, u32[]{:S(2)}, u32[]{:S(2)}) %all-to-all-start.2) | async-done | bytes 6176 | tf_op jit(solution)/shard_map/all_to_all | solution.py:53
  336.9 0.3 convolution_bitcast_fusion
  337.2 0.1 copy.59
  337.3 0.6 fusion.5
  337.9 0.7 copy.60
  (6 shorter events, 0.0 us)
Async XLA Ops:
  7.2 15.3 %all-gather.2.cloned.1.call-start = ((), (), s32[]{:S(2)}) async-start(), calls=%async_computation.3 | async-start | bytes 2752512 | tf_op jit(solution)/shard_map/all_gather | solution.py:36
  11.6 31.9 %all-to-all-start = ((bf16[16,48,2]{1,2,0:T(2,128)(2,1)}), bf16[16,48,2]{1,2,0:T(2,128)(2,1)S(1)}, u32[]{:S(2)}, u32[]{:S(2)}) async-start(bf16[16,48,2]{1,2,0:T(2,128)(2,1)} %convolution_convert_fusion), calls=%async_computation | async-start | bytes 16384 | tf_op jit(solution)/shard_map/all_to_all | solution.py:40
  43.4 7.0 %copy-start = (bf16[2,768,512]{2,1,0:T(8,128)(2,1)S(1)}, bf16[2,768,512]{2,1,0:T(8,128)(2,1)}, u32[]{:S(2)}) copy-start(bf16[2,768,512]{2,1,0:T(8,128)(2,1)} %param.9) | copy-start | bytes 4718596
  43.4 215.5 %all-to-all-start.1 = ((bf16[16,48,7168]{2,1,0:T(8,128)(2,1)}), bf16[16,48,7168]{2,1,0:T(8,128)(2,1)}, u32[]{:S(2)}, u32[]{:S(2)}) async-start(bf16[16,48,7168]{2,1,0:T(8,128)(2,1)} %broadcast_select_fusion), calls=%async_computation.1 | async-start | bytes 22020096 | tf_op jit(solution)/shard_map/all_to_all | solution.py:39
  281.1 55.8 %all-to-all-start.2 = ((f32[16,48,2]{1,2,0:T(2,128)}), f32[16,48,2]{1,2,0:T(2,128)S(1)}, u32[]{:S(2)}, u32[]{:S(2)}) async-start(f32[16,48,2]{1,2,0:T(2,128)} %copy.58), calls=%async_computation.2 | async-start | bytes 32768 | tf_op jit(solution)/shard_map/all_to_all | solution.py:53
Sparse Core Ops, SparseCore 0:
  9.5 12.8 all-gather.1
where the time goes:
time: 346 us; the launch traced here: 345 us
  waiting for transfers between devices  216 us (62%)
  starting transfers between devices  63.8 us (18%)
  matrix products  20.4 us (6%)
  local copies, waits for them, and re-layouts  16.8 us (5%)
  between operations  14.2 us (4%)
  other arithmetic  11 us (3%)
    all_to_all x1, waiting for transfers between devices, on_device(): lax.all_to_all(rows_send, 'node', split_axis=0, concat_axis=0, tiled=True)  208 us
    all_to_all x1, starting transfers between devices, on_device(): lax.all_to_all(summed, 'node', split_axis=0, concat_axis=0, tiled=True)  48.5 us
    dot_general x1, matrix products, on_device(): jnp.einsum('rd,ehd->erh', rows_in.reshape(slot_rows, -1), weight_down, pr...  18.1 us
    select_n x2, other arithmetic, gather_slots(): return jnp.take(padded, index, axis=0)  9.88 us
    gather x1, local copies, waits for them, and re-layouts, gather_slots(): return jnp.take(padded, index, axis=0)  9.4 us
    all_to_all x1, starting transfers between devices, on_device(): lax.all_to_all(prob_send, 'node', split_axis=0, concat_axis=0, tiled=True)  8.31 us
    all_to_all x1, starting transfers between devices, on_device(): lax.all_to_all(rows_send, 'node', split_axis=0, concat_axis=0, tiled=True)  6.96 us
  transfers between devices with their start and end apart: 4, of which 3 were waited for; matrix products, arithmetic and copies ran while one was open for 8% of the time, Pallas kernels for 0%

commit v1 on v0

--- a/solution.py
+++ b/solution.py
@@ -1,7 +1,18 @@
+import functools
+
 import jax
 import jax.numpy as jnp
 from jax import lax
+from jax.experimental import pallas as pl
+from jax.experimental.pallas import tpu as pltpu
 from jax.sharding import PartitionSpec as P
+
+MESH = pl.DeviceIdType.MESH
+PLANES = 4
+SIDE = 4
+F32 = jnp.float32
+BF16 = jnp.bfloat16
+NT = (((1,), (1,)), ((), ()))
 
 
 def gather_slots(source, source_row, slot_valid):
@@ -10,7 +21,7 @@
     return jnp.take(padded, index, axis=0)
 
 
-def on_device(grad_out, probs, node_list, weight_down, saved_hidden):
+def plain(grad_out, probs, node_list, weight_down, saved_hidden):
     node_count = lax.axis_size("node")
     tok_rows = node_list.shape[0]
     route_count = node_list.shape[1]
@@ -33,17 +44,14 @@
     prob_send = jnp.einsum(
         "tms,tmc->msc", select_full, picked, precision=lax.Precision.HIGHEST
     ).astype(jnp.bfloat16)
-    full_rows = lax.all_gather(grad_out, "local", axis=1, tiled=True)
-    rows_send = gather_slots(full_rows, source_row, slot_valid)
+    rows_send = gather_slots(grad_out, source_row, slot_valid)
     rows_in, prob_in = (
         lax.all_to_all(rows_send, "node", split_axis=0, concat_axis=0, tiled=True),
         lax.all_to_all(prob_send, "node", split_axis=0, concat_axis=0, tiled=True),
     )
+    rows_in = lax.all_gather(rows_in.reshape(slot_rows, -1), "local", axis=1, tiled=True)
     hidden_grads = jnp.einsum(
-        "rd,ehd->erh",
-        rows_in.reshape(slot_rows, -1),
-        weight_down,
-        preferred_element_type=jnp.float32,
+        "rd,ehd->erh", rows_in, weight_down, preferred_element_type=jnp.float32
     )
     scales = jnp.transpose(prob_in.reshape(slot_rows, expert_count).astype(jnp.float32))
     grad_hidden = (scales[:, :, None] * hidden_grads).astype(jnp.bfloat16)
@@ -54,6 +62,455 @@
     per_node = jnp.einsum("tms,msc->tmc", select_full, returned, precision=lax.Precision.HIGHEST)
     grad_probs = jnp.einsum("tjm,tmc->tjc", listed, per_node, precision=lax.Precision.HIGHEST)
     return (grad_hidden, grad_probs.reshape(tok_rows, route_count * expert_count))
+
+
+def fused_kernel(
+    chunks, go_ref, pr_ref, nl_ref, w_ref, sh_ref, out_ref, gp_ref,
+    zbuf, aux, auxf, smat, sbuf, psend, rbuf, pbuf, wv, hv, acc, obuf, part, ret, home, onehot,
+    in_sem, w_sem, h_sem, o_sem, z_recv, z_up, z_down, a_recv, a_up, a_down,
+    r_send, r_recv, p_send, p_recv, s_send, s_recv, t_send, t_recv,
+):
+    node, core = lax.axis_index("node"), lax.axis_index("local")
+    z, q = node // SIDE, node % SIDE
+    x, y = q % 2, q // 2
+    cap, width = rbuf.shape[4], rbuf.shape[5]
+    toks = zbuf.shape[2]
+    hid = hv.shape[3]
+    units = PLANES * chunks
+    other = 1 - core
+    total = PLANES * SIDE * 2
+    me = node * 2 + core
+
+    barrier = pltpu.get_barrier_semaphore()
+
+    def greet(i, carry):
+        peer = (me + i) % total
+        pl.semaphore_signal(barrier, inc=1, device_id=(peer // 2, peer % 2), device_id_type=MESH)
+        return carry
+
+    lax.fori_loop(1, total, greet, 0)
+
+    def load_in(ch):
+        return pltpu.make_async_copy(go_ref.at[:, pl.ds(ch * width, width)], zbuf.at[z, ch], in_sem.at[ch])
+
+    def load_w(h, ch):
+        return pltpu.make_async_copy(
+            w_ref.at[:, pl.ds((h * chunks + ch) * width, width)], wv.at[h, ch], w_sem.at[h, ch]
+        )
+
+    load_h = pltpu.make_async_copy(sh_ref, hv, h_sem)
+    for ch in range(chunks):
+        load_in(ch).start()
+    for ch in range(chunks):
+        for h in range(2):
+            load_w(h, ch).start()
+    load_h.start()
+
+    nodes = PLANES * SIDE
+    rows_m = lax.broadcasted_iota(jnp.int32, (nodes, toks), 0)
+    member = jnp.zeros((nodes, toks), F32)
+    first = jnp.zeros((nodes, toks), F32)
+    second = jnp.zeros((nodes, toks), F32)
+    hits = []
+    for j in range(4):
+        hit = (nl_ref[j:j + 1, :] == rows_m).astype(F32)
+        hits.append(hit)
+        member = member + hit
+        first = first + hit * pr_ref[2 * j:2 * j + 1, :].astype(F32)
+        second = second + hit * pr_ref[2 * j + 1:2 * j + 2, :].astype(F32)
+    before = (
+        lax.broadcasted_iota(jnp.int32, (toks, toks), 0) < lax.broadcasted_iota(jnp.int32, (toks, toks), 1)
+    ).astype(F32).astype(BF16)
+    arrival = jnp.dot(member.astype(BF16), before, preferred_element_type=F32)
+    slot_of = jnp.where(member > 0.5, arrival, -1.0)
+    aux[z] = jnp.concatenate([slot_of, first, second], axis=0).astype(BF16)
+    tall = jnp.concatenate(
+        [nl_ref[...].astype(F32)]
+        + [jnp.sum(hits[j] * slot_of, axis=0, keepdims=True) for j in range(4)]
+        + [jnp.zeros((toks - 8, toks), F32)],
+        axis=0,
+    ).T
+    home[...] = tall
+    lane = lax.broadcasted_iota(jnp.int32, (toks, toks), 1)
+    lane_node = (lane % nodes).astype(F32)
+    for j in range(4):
+        onehot[j] = jnp.where((lane < 3 * nodes) & (tall[:, j:j + 1] == lane_node), 1.0, 0.0).astype(BF16)
+
+    pl.semaphore_wait(barrier, total - 1)
+
+    def unit(u):
+        k0, c0 = u // chunks, u % chunks
+        v = u - chunks
+        mixed = ((z == 1) | (z == 2)) & (k0 >= 1) & (k0 <= 2)
+        k = jnp.where(mixed, 1 + v % 2, k0)
+        ch = jnp.where(mixed, v // 2, c0)
+        near = z + 1 - 2 * (z % 2)
+        low = z < 2
+        zb = jnp.where(
+            k == 0, z, jnp.where(k == 1, near, jnp.where(k == 2, jnp.where(low, 2, 1), jnp.where(low, 3, 0)))
+        )
+        return k, ch, zb
+
+    def mate(d):
+        return (x + d % 2) % 2 + 2 * ((y + d // 2) % 2)
+
+    def along(ref, index, send, recv, step):
+        return pltpu.make_async_remote_copy(
+            src_ref=ref.at[index], dst_ref=ref.at[index], send_sem=send.at[index], recv_sem=recv.at[index],
+            device_id=(node + step * SIDE, core), device_id_type=MESH,
+        )
+
+    def hop(zb, ch, step):
+        return along(zbuf, (zb, ch), z_up if step > 0 else z_down, z_recv, step)
+
+    def hop_aux(zb, step):
+        return along(aux, zb, a_up if step > 0 else a_down, a_recv, step)
+
+    def pack(zb, ch, d):
+        return pltpu.make_async_remote_copy(
+            src_ref=sbuf.at[zb, ch, d - 1], dst_ref=rbuf.at[core, ch, zb, q],
+            send_sem=r_send.at[zb, ch, d - 1], recv_sem=r_recv.at[zb, ch, d - 1],
+            device_id=(z * SIDE + mate(d), core), device_id_type=MESH,
+        )
+
+    def pack_in(zb, ch, d):
+        return pltpu.make_async_remote_copy(
+            src_ref=sbuf.at[zb, ch, d - 1], dst_ref=rbuf.at[core, ch, zb, mate(d)],
+            send_sem=r_send.at[zb, ch, d - 1], recv_sem=r_recv.at[zb, ch, d - 1],
+            device_id=(z * SIDE + mate(d), core), device_id_type=MESH,
+        )
+
+    def scale(zb, d):
+        return pltpu.make_async_remote_copy(
+            src_ref=psend.at[zb, d - 1], dst_ref=pbuf.at[zb, q],
+            send_sem=p_send.at[zb, d - 1], recv_sem=p_recv.at[zb, d - 1],
+            device_id=(z * SIDE + mate(d), core), device_id_type=MESH,
+        )
+
+    def scale_in(zb, d):
+        return pltpu.make_async_remote_copy(
+            src_ref=psend.at[zb, d - 1], dst_ref=pbuf.at[zb, mate(d)],
+            send_sem=p_send.at[zb, d - 1], recv_sem=p_recv.at[zb, d - 1],
+            device_id=(z * SIDE + mate(d), core), device_id_type=MESH,
+        )
+
+    def share(half, zb, ch):
+        return pltpu.make_async_remote_copy(
+            src_ref=rbuf.at[half, ch, zb], dst_ref=rbuf.at[half, ch, zb],
+            send_sem=s_send.at[zb, ch], recv_sem=s_recv.at[zb, ch],
+            device_id=(node, other), device_id_type=MESH,
+        )
+
+    def give(zb, d, dc):
+        target = zb * SIDE + mate(d)
+        return pltpu.make_async_remote_copy(
+            src_ref=part.at[zb, d], dst_ref=ret.at[node, core],
+            send_sem=t_send.at[zb, d, dc], recv_sem=t_recv.at[node, core],
+            device_id=(target, (core + dc) % 2), device_id_type=MESH,
+        )
+
+    def give_in(m, c):
+        return pltpu.make_async_remote_copy(
+            src_ref=part.at[0, 0], dst_ref=ret.at[m, c],
+            send_sem=t_send.at[0, 0, 0], recv_sem=t_recv.at[m, c],
+            device_id=(node, other), device_id_type=MESH,
+        )
+
+    def store(zb, e):
+        return pltpu.make_async_copy(obuf.at[zb, e], out_ref.at[e, zb], o_sem.at[zb, e])
+
+    cap_rows = lax.broadcasted_iota(jnp.int32, (cap, toks), 0).astype(F32)
+    cap_lane = lax.broadcasted_iota(jnp.int32, (cap, 128), 1)
+
+    def stage_a(u):
+        k, ch, zb = unit(u)
+
+        @pl.when(k == 0)
+        def _():
+            load_in(ch).wait()
+
+        @pl.when(k > 0)
+        def _():
+            @pl.when(ch == 0)
+            def _():
+                hop_aux(zb, 1).wait_recv()
+
+            hop(zb, ch, 1).wait_recv()
+
+        for step, go in ((1, (zb <= z) & (z < PLANES - 1)), (-1, (zb >= z) & (z > 0))):
+            @pl.when(go)
+            def _(step=step):
+                @pl.when(ch == 0)
+                def _():
+                    hop_aux(zb, step).start()
+
+                hop(zb, ch, step).start()
+
+        @pl.when(ch == 0)
+        def _():
+            auxf[...] = aux[zb].astype(F32)
+            for d in (3, 1, 2, 0):
+                m = z * SIDE + mate(d)
+                sel = (auxf[pl.ds(m, 1), :] == cap_rows).astype(F32)
+                smat[zb, d] = sel.astype(BF16)
+                col0 = jnp.sum(sel * auxf[pl.ds(nodes + m, 1), :], axis=1, keepdims=True)
+                col1 = jnp.sum(sel * auxf[pl.ds(2 * nodes + m, 1), :], axis=1, keepdims=True)
+                value = jnp.where(cap_lane == 0, col0, jnp.where(cap_lane == 1, col1, 0.0)).astype(BF16)
+                if d:
+                    psend[zb, d - 1] = value
+                    scale(zb, d).start()
+                else:
+                    pbuf[zb, q] = value
+
+        for d in (3, 1, 2, 0):
+            value = jnp.dot(smat[zb, d], zbuf[zb, ch], preferred_element_type=F32).astype(BF16)
+            if d:
+                sbuf[zb, ch, d - 1] = value
+                pack(zb, ch, d).start()
+            else:
+                rbuf[core, ch, zb, q] = value
+
+    def stage_b(u):
+        k, ch, zb = unit(u)
+        for d in (1, 2, 3):
+            pack_in(zb, ch, d).wait_recv()
+
+        share(core, zb, ch).start()
+
+    def stage_c(u):
+        k, ch, zb = unit(u)
+        share(other, zb, ch).wait_recv()
+
+        @pl.when(ch == 0)
+        def _():
+            acc[zb] = jnp.zeros(acc.shape[1:], F32)
+
+        left = rbuf[0, ch, zb].reshape(SIDE * cap, width)
+        right = rbuf[1, ch, zb].reshape(SIDE * cap, width)
+        tile = min(256, hid)
+        for n in range(2 * hid // tile):
+            cols = slice(n * tile, (n + 1) * tile)
+            acc[zb, :, cols] += (
+                lax.dot_general(left, wv[0, ch, cols, :], NT, preferred_element_type=F32)
+                + lax.dot_general(right, wv[1, ch, cols, :], NT, preferred_element_type=F32)
+            )
+
+        @pl.when(ch == chunks - 1)
+        def _():
+            for d in (1, 2, 3):
+                scale_in(zb, d).wait_recv()
+            scales = pbuf[zb].reshape(SIDE * cap, 128).astype(F32)
+            folded = []
+            for e in range(2):
+                g = acc[zb, :, e * hid:(e + 1) * hid]
+                prod = hv[e, zb].astype(F32) * g
+                fold = prod[:, :128]
+                for b in range(1, hid // 128):
+                    fold = fold + prod[:, b * 128:(b + 1) * 128]
+                folded.append(fold)
+                obuf[zb, e] = (scales[:, e:e + 1] * g).astype(BF16)
+                store(zb, e).start()
+            fill = jnp.zeros((128 - 2 * cap, 128), F32)
+            for s in range(SIDE):
+                rows = slice(s * cap, (s + 1) * cap)
+                sums = jnp.sum(
+                    jnp.concatenate([folded[0][rows], folded[1][rows], fill], axis=0).T, axis=0, keepdims=True
+                )
+                for d in range(SIDE):
+                    @pl.when(mate(d) == s)
+                    def _(d=d, sums=sums):
+                        part[zb, d] = jnp.broadcast_to(sums, (8, 128))
+            for d in range(SIDE):
+                for dc in range(2):
+                    if d == 0 and dc == 0:
+                        @pl.when(zb != z)
+                        def _():
+                            give(zb, 0, 0).start()
+
+                        @pl.when(zb == z)
+                        def _():
+                            ret[node, core] = part[zb, 0]
+                    else:
+                        give(zb, d, dc).start()
+
+    def body(it, carry):
+        @pl.when(it < units)
+        def _():
+            stage_a(it)
+
+        @pl.when(it == 2)
+        def _():
+            for ch in range(chunks):
+                for h in range(2):
+                    load_w(h, ch).wait()
+            load_h.wait()
+
+        @pl.when(it >= 2)
+        def _():
+            stage_c(it - 2)
+
+        @pl.when((it >= 1) & (it <= units))
+        def _():
+            stage_b(it - 1)
+
+        return carry
+
+    lax.fori_loop(0, units + 2, body, 0)
+
+    def finish_block(zb, carry):
+        for e in range(2):
+            store(zb, e).wait()
+        for step, go in ((1, (zb <= z) & (z < PLANES - 1)), (-1, (zb >= z) & (z > 0))):
+            @pl.when(go)
+            def _(step=step):
+                hop_aux(zb, step).wait_send()
+
+        for d in range(1, SIDE):
+            scale(zb, d).wait_send()
+        for d in range(SIDE):
+            for dc in range(2):
+                if d == 0 and dc == 0:
+                    @pl.when(zb != z)
+                    def _():
+                        give(zb, 0, 0).wait_send()
+                else:
+                    give(zb, d, dc).wait_send()
+
+        def finish_unit(ch, inner):
+            for step, go in ((1, (zb <= z) & (z < PLANES - 1)), (-1, (zb >= z) & (z > 0))):
+                @pl.when(go)
+                def _(step=step):
+                    hop(zb, ch, step).wait_send()
+
+            for d in range(1, SIDE):
+                pack(zb, ch, d).wait_send()
+            share(core, zb, ch).wait_send()
+            return inner
+
+        return lax.fori_loop(0, chunks, finish_unit, carry)
+
+    lax.fori_loop(0, PLANES, finish_block, 0)
+
+    def arrive(i, carry):
+        peer = (me + i) % total
+        give_in(peer // 2, peer % 2).wait_recv()
+        return carry
+
+    lax.fori_loop(1, total, arrive, 0)
+
+    sub = lax.broadcasted_iota(jnp.int32, (8, 128), 0)
+    halves = []
+    for base in range(0, nodes, 8):
+        rows = jnp.zeros((8, 128), F32)
+        for m in range(8):
+            rows = jnp.where(sub == m, ret[base + m, 0] + ret[base + m, 1], rows)
+        halves.append(rows)
+    sums = jnp.concatenate(halves, axis=0)
+    high = sums.astype(BF16).astype(F32)
+    rest = sums - high
+    middle = rest.astype(BF16).astype(F32)
+    parts = jnp.concatenate(
+        [high, middle, rest - middle, jnp.zeros((128 - 3 * nodes, 128), F32)], axis=0
+    ).astype(BF16)
+    lanes = lax.broadcasted_iota(jnp.int32, (toks, 128), 1)
+    lanes_f = lanes.astype(F32)
+    result = jnp.zeros((toks, 128), F32)
+    for j in range(4):
+        picked = jnp.dot(onehot[j], parts, preferred_element_type=F32)
+        slot = home[:, 4 + j:5 + j]
+        for e in range(2):
+            column = jnp.sum(jnp.where(lanes_f == slot + float(e * cap), picked, 0.0), axis=1, keepdims=True)
+            result = jnp.where(lanes == 2 * j + e, column, result)
+    gp_ref[...] = result.T[:8, :]
+
+
+def fused(chunks, grad_out, probs, node_list, weight_down, saved_hidden):
+    toks, half = grad_out.shape
+    width = half // chunks
+    experts, hid, full = weight_down.shape
+    slots = saved_hidden.shape[1]
+    cap = slots // (PLANES * SIDE)
+    group = SIDE * cap
+    dma = pltpu.SemaphoreType.DMA
+    anywhere = pl.BlockSpec(memory_space=pl.ANY)
+    vmem = pl.BlockSpec(memory_space=pltpu.VMEM)
+    out, gp = pl.pallas_call(
+        functools.partial(fused_kernel, chunks),
+        out_shape=(
+            jax.ShapeDtypeStruct((experts, PLANES, group, hid), BF16),
+            jax.ShapeDtypeStruct((8, toks), F32),
+        ),
+        in_specs=[anywhere, vmem, vmem, anywhere, anywhere],
+        out_specs=(anywhere, vmem),
+        scratch_shapes=[
+            pltpu.VMEM((PLANES, chunks, toks, width), BF16),
+            pltpu.VMEM((PLANES, 48, toks), BF16),
+            pltpu.VMEM((48, toks), F32),
+            pltpu.VMEM((PLANES, SIDE, cap, toks), BF16),
+            pltpu.VMEM((PLANES, chunks, 3, cap, width), BF16),
+            pltpu.VMEM((PLANES, 3, cap, 128), BF16),
+            pltpu.VMEM((2, chunks, PLANES, SIDE, cap, width), BF16),
+            pltpu.VMEM((PLANES, SIDE, cap, 128), BF16),
+            pltpu.VMEM((2, chunks, experts * hid, width), BF16),
+            pltpu.VMEM((experts, PLANES, group, hid), BF16),
+            pltpu.VMEM((PLANES, group, experts * hid), F32),
+            pltpu.VMEM((PLANES, experts, group, hid), BF16),
+            pltpu.VMEM((PLANES, SIDE, 8, 128), F32),
+            pltpu.VMEM((PLANES * SIDE, 2, 8, 128), F32),
+            pltpu.VMEM((toks, toks), F32),
+            pltpu.VMEM((4, toks, toks), BF16),
+            dma((chunks,)),
+            dma((2, chunks)),
+            dma(()),
+            dma((PLANES, 2)),
+            dma((PLANES, chunks)),
+            dma((PLANES, chunks)),
+            dma((PLANES, chunks)),
+            dma((PLANES,)),
+            dma((PLANES,)),
+            dma((PLANES,)),
+            dma((PLANES, chunks, 3)),
+            dma((PLANES, chunks, 3)),
+            dma((PLANES, 3)),
+            dma((PLANES, 3)),
+            dma((PLANES, chunks)),
+            dma((PLANES, chunks)),
+            dma((PLANES, SIDE, 2)),
+            dma((PLANES * SIDE, 2)),
+        ],
+        compiler_params=pltpu.CompilerParams(
+            collective_id=0, has_side_effects=True, vmem_limit_bytes=56 * 2**20
+        ),
+        cost_estimate=pl.CostEstimate(
+            flops=2 * slots * full * experts * hid, bytes_accessed=2 * experts * hid * full, transcendentals=0
+        ),
+    )(
+        grad_out,
+        probs.T,
+        node_list.T,
+        weight_down.reshape(experts * hid, full),
+        saved_hidden.reshape(experts, PLANES, group, hid),
+    )
+    return out.reshape(experts, slots, hid), gp.T
+
+
+def on_device(*args):
+    grad_out, probs, node_list, weight_down, saved_hidden = args
+    nodes, cores = lax.axis_size("node"), lax.axis_size("local")
+    cap = saved_hidden.shape[1] // nodes
+    suits = (
+        nodes == PLANES * SIDE
+        and cores == 2
+        and cap % 16 == 0
+        and 2 * cap <= 128
+        and node_list.shape == (128, 4)
+        and weight_down.shape[0] == 2
+        and weight_down.shape[1] % 128 == 0
+        and grad_out.shape[1] % 512 == 0
+    )
+    if suits:
+        return fused(4, *args)
+    return plain(*args)
 
 
 def solution(mesh):

time: 346 us -> 98.4 us (0.28)
  waiting for transfers between devices: 216 us -> 0 us
  Pallas kernels: 0 us -> 94.4 us
  starting transfers between devices: 63.8 us -> 0 us
  matrix products: 20.4 us -> 0 us
  local copies, waits for them, and re-layouts: 16.8 us -> 3.25 us
  between operations: 14.2 us -> 0.65 us
  other arithmetic: 11 us -> 0 us
    all_to_all x3 -> x0, waiting for transfers between devices: 213 us -> none  [the longest x1 208 us: on_device(): lax.all_to_all(rows_send, 'node', split_axis=0, concat_axis=0, tiled=True)]
    pallas_call x0 -> x1, Pallas kernels: none -> 94.4 us  [fused(): pl.pallas_call(functools.partial(fused_kernel, chunks), out_shape=(jax.Sh...]
    all_to_all x3 -> x0, starting transfers between devices: 63.7 us -> none  [the longest x1 48.5 us: on_device(): lax.all_to_all(summed, 'node', split_axis=0, concat_axis=0, tiled=True)]
    dot_general x5 -> x0, matrix products: 20.4 us -> none  [the longest x1 18.1 us: on_device(): jnp.einsum('rd,ehd->erh', rows_in.reshape(slot_rows, -1), weight_down, pr...]
    select_n x2 -> x0, other arithmetic: 9.88 us -> none  [gather_slots(): return jnp.take(padded, index, axis=0)]
    gather x1 -> x0, local copies, waits for them, and re-layouts: 9.4 us -> none  [gather_slots(): return jnp.take(padded, index, axis=0)]
  transfers between devices with their start and end apart: 4 -> 0, of which waited for: 3 -> 0; matrix products, arithmetic and copies ran while one was open for 8% -> 0% of each run, Pallas kernels for 0% -> 0%
where the time goes in v1:
time: 98.4 us; the launch traced here: 98.3 us
  Pallas kernels  94.4 us (96%)
  local copies, waits for them, and re-layouts  3.25 us (3%)
    pallas_call x1, Pallas kernels, fused(): pl.pallas_call(functools.partial(fused_kernel, chunks), out_shape=(jax.Sh...  94.4 us
    unnamed x4, local copies, waits for them, and re-layouts  3.25 us

profile of v1, /device:TPU:0, one launch (start us, length us, event | category | flops | bytes accessed | tf_op | source)
XLA Modules:
  0.0 98.3 jit_solution(8233311699978850180)
XLA Ops:
  0.6 94.4 %shard_map.68 = (bf16[2,4,192,512]{3,2,1,0:T(8,128)(2,1)}, f32[8,128]{1,0:T(8,128)}) custom-call(bf16[128,3584]{1,0:T(8,128)(2,1)} %go_ref.1, bf16[8,128]{1,0:T(8,128)(2,1)} %bitcast.10, s32[4,128]{1,0:T(4,128)} %bitcast.11, bf16[1024,7168]{1,0:T(8,128)(2,1)} %bitcast.8, bf16[2,4,192,512]{3,2,1,0:T(8,128)(2,1)} %bitcast.9), custom_call_target="tpu_custom_call" | custom-call | flops 11274289152 | bytes 14680064 | tf_op jit(solution)/shard_map/pallas_call | solution.py:437
  95.0 0.0 copy-start
  95.0 2.7 %copy.9 = bf16[2,768,512]{2,1,0:T(8,128)(2,1)} copy(bf16[2,768,512]{2,1,0:T(8,128)(2,1)} %bitcast.6) | data formatting | bytes 3145728
  97.7 0.0 copy-done
  97.7 0.6 copy.10
Async XLA Ops:
  95.0 2.7 %copy-start = (f32[8,128]{1,0:T(8,128)S(1)}, f32[8,128]{1,0:T(8,128)}, u32[]{:S(2)}) copy-start(f32[8,128]{1,0:T(8,128)} %get-tuple-element.5) | copy-start | bytes 12292

commit v2 on v1

--- a/solution.py
+++ b/solution.py
@@ -95,7 +95,8 @@
 
     def load_w(h, ch):
         return pltpu.make_async_copy(
-            w_ref.at[:, pl.ds((h * chunks + ch) * width, width)], wv.at[h, ch], w_sem.at[h, ch]
+            w_ref.at[:, pl.ds((h * chunks + ch) * width, width)], wv.at[ch, :, pl.ds(h * width, width)],
+            w_sem.at[h, ch],
         )
 
     load_h = pltpu.make_async_copy(sh_ref, hv, h_sem)
@@ -262,8 +263,11 @@
                 else:
                     pbuf[zb, q] = value
 
+        packs = jnp.dot(
+            smat[zb].reshape(SIDE * cap, toks), zbuf[zb, ch], preferred_element_type=F32
+        ).astype(BF16)
         for d in (3, 1, 2, 0):
-            value = jnp.dot(smat[zb, d], zbuf[zb, ch], preferred_element_type=F32).astype(BF16)
+            value = packs[d * cap:(d + 1) * cap]
             if d:
                 sbuf[zb, ch, d - 1] = value
                 pack(zb, ch, d).start()
@@ -285,15 +289,13 @@
         def _():
             acc[zb] = jnp.zeros(acc.shape[1:], F32)
 
-        left = rbuf[0, ch, zb].reshape(SIDE * cap, width)
-        right = rbuf[1, ch, zb].reshape(SIDE * cap, width)
+        rows_in = jnp.concatenate(
+            [rbuf[h, ch, zb].reshape(SIDE * cap, width) for h in range(2)], axis=1
+        )
         tile = min(256, hid)
         for n in range(2 * hid // tile):
             cols = slice(n * tile, (n + 1) * tile)
-            acc[zb, :, cols] += (
-                lax.dot_general(left, wv[0, ch, cols, :], NT, preferred_element_type=F32)
-                + lax.dot_general(right, wv[1, ch, cols, :], NT, preferred_element_type=F32)
-            )
+            acc[zb, :, cols] += lax.dot_general(rows_in, wv[ch, cols, :], NT, preferred_element_type=F32)
 
         @pl.when(ch == chunks - 1)
         def _():
@@ -333,6 +335,10 @@
                     else:
                         give(zb, d, dc).start()
 
+    far = 2 * chunks + 2
+    between = (z == 1) | (z == 2)
+    lag = jnp.where(between, far, 2)
+
     def body(it, carry):
         @pl.when(it < units)
         def _():
@@ -345,9 +351,9 @@
                     load_w(h, ch).wait()
             load_h.wait()
 
-        @pl.when(it >= 2)
-        def _():
-            stage_c(it - 2)
+        @pl.when((it >= lag) & (it < units + lag))
+        def _():
+            stage_c(it - lag)
 
         @pl.when((it >= 1) & (it <= units))
         def _():
@@ -355,7 +361,7 @@
 
         return carry
 
-    lax.fori_loop(0, units + 2, body, 0)
+    lax.fori_loop(0, units + jnp.where(between, far, 2), body, 0)
 
     def finish_block(zb, carry):
         for e in range(2):
@@ -451,7 +457,7 @@
             pltpu.VMEM((PLANES, 3, cap, 128), BF16),
             pltpu.VMEM((2, chunks, PLANES, SIDE, cap, width), BF16),
             pltpu.VMEM((PLANES, SIDE, cap, 128), BF16),
-            pltpu.VMEM((2, chunks, experts * hid, width), BF16),
+            pltpu.VMEM((chunks, experts * hid, 2 * width), BF16),
             pltpu.VMEM((experts, PLANES, group, hid), BF16),
             pltpu.VMEM((PLANES, group, experts * hid), F32),
             pltpu.VMEM((PLANES, experts, group, hid), BF16),

time: 98.4 us -> 98.5 us (level)
  no operation moved by 1% of the time
where the time goes in v2:
time: 98.5 us; the launch traced here: 98.3 us
  Pallas kernels  94.4 us (96%)
  local copies, waits for them, and re-layouts  3.25 us (3%)
    pallas_call x1, Pallas kernels, fused(): pl.pallas_call(functools.partial(fused_kernel, chunks), out_shape=(jax.Sh...  94.4 us
    unnamed x4, local copies, waits for them, and re-layouts  3.25 us

profile of v2, /device:TPU:0, one launch (start us, length us, event | category | flops | bytes accessed | tf_op | source)
XLA Modules:
  0.0 98.3 jit_solution(4190671446488243434)
XLA Ops:
  0.6 94.4 %shard_map.68 = (bf16[2,4,192,512]{3,2,1,0:T(8,128)(2,1)}, f32[8,128]{1,0:T(8,128)}) custom-call(bf16[128,3584]{1,0:T(8,128)(2,1)} %go_ref.1, bf16[8,128]{1,0:T(8,128)(2,1)} %bitcast.10, s32[4,128]{1,0:T(4,128)} %bitcast.11, bf16[1024,7168]{1,0:T(8,128)(2,1)} %bitcast.8, bf16[2,4,192,512]{3,2,1,0:T(8,128)(2,1)} %bitcast.9), custom_call_target="tpu_custom_call" | custom-call | flops 11274289152 | bytes 14680064 | tf_op jit(solution)/shard_map/pallas_call | solution.py:443
  95.0 0.0 copy-start
  95.0 2.7 %copy.9 = bf16[2,768,512]{2,1,0:T(8,128)(2,1)} copy(bf16[2,768,512]{2,1,0:T(8,128)(2,1)} %bitcast.6) | data formatting | bytes 3145728
  97.7 0.0 copy-done
  97.7 0.6 copy.10
Async XLA Ops:
  95.0 2.7 %copy-start = (f32[8,128]{1,0:T(8,128)S(1)}, f32[8,128]{1,0:T(8,128)}, u32[]{:S(2)}) copy-start(f32[8,128]{1,0:T(8,128)} %get-tuple-element.5) | copy-start | bytes 12292

commit v3 on v2

--- a/solution.py
+++ b/solution.py
@@ -139,18 +139,20 @@
 
     pl.semaphore_wait(barrier, total - 1)
 
+    def block(k):
+        near = z + 1 - 2 * (z % 2)
+        low = z < 2
+        return jnp.where(
+            k == 0, z, jnp.where(k == 1, near, jnp.where(k == 2, jnp.where(low, 2, 1), jnp.where(low, 3, 0)))
+        )
+
     def unit(u):
         k0, c0 = u // chunks, u % chunks
         v = u - chunks
         mixed = ((z == 1) | (z == 2)) & (k0 >= 1) & (k0 <= 2)
         k = jnp.where(mixed, 1 + v % 2, k0)
         ch = jnp.where(mixed, v // 2, c0)
-        near = z + 1 - 2 * (z % 2)
-        low = z < 2
-        zb = jnp.where(
-            k == 0, z, jnp.where(k == 1, near, jnp.where(k == 2, jnp.where(low, 2, 1), jnp.where(low, 3, 0)))
-        )
-        return k, ch, zb
+        return k, ch, block(k)
 
     def mate(d):
         return (x + d % 2) % 2 + 2 * ((y + d // 2) % 2)
@@ -335,35 +337,8 @@
                     else:
                         give(zb, d, dc).start()
 
-    far = 2 * chunks + 2
-    between = (z == 1) | (z == 2)
-    lag = jnp.where(between, far, 2)
-
-    def body(it, carry):
-        @pl.when(it < units)
-        def _():
-            stage_a(it)
-
-        @pl.when(it == 2)
-        def _():
-            for ch in range(chunks):
-                for h in range(2):
-                    load_w(h, ch).wait()
-            load_h.wait()
-
-        @pl.when((it >= lag) & (it < units + lag))
-        def _():
-            stage_c(it - lag)
-
-        @pl.when((it >= 1) & (it <= units))
-        def _():
-            stage_b(it - 1)
-
-        return carry
-
-    lax.fori_loop(0, units + jnp.where(between, far, 2), body, 0)
-
-    def finish_block(zb, carry):
+    def finish_block(k, carry):
+        zb = block(k)
         for e in range(2):
             store(zb, e).wait()
         for step, go in ((1, (zb <= z) & (z < PLANES - 1)), (-1, (zb >= z) & (z > 0))):
@@ -395,7 +370,39 @@
 
         return lax.fori_loop(0, chunks, finish_unit, carry)
 
-    lax.fori_loop(0, PLANES, finish_block, 0)
+    between = (z == 1) | (z == 2)
+    swap = jnp.where(between, chunks // 2 + 1, 1)
+    lag = jnp.where(between, chunks + 1, 2)
+
+    def body(it, carry):
+        @pl.when(it == units + lag - 3)
+        def _():
+            lax.fori_loop(0, 2, finish_block, 0)
+
+        @pl.when(it < units)
+        def _():
+            stage_a(it)
+
+        @pl.when(it == 2)
+        def _():
+            for ch in range(chunks):
+                for h in range(2):
+                    load_w(h, ch).wait()
+            load_h.wait()
+
+        @pl.when((it >= lag) & (it < units + lag))
+        def _():
+            stage_c(it - lag)
+
+        @pl.when((it >= swap) & (it < units + swap))
+        def _():
+            stage_b(it - swap)
+
+        return carry
+
+    lax.fori_loop(0, units + lag, body, 0)
+
+    lax.fori_loop(2, PLANES, finish_block, 0)
 
     def arrive(i, carry):
         peer = (me + i) % total
@@ -512,10 +519,10 @@
         and node_list.shape == (128, 4)
         and weight_down.shape[0] == 2
         and weight_down.shape[1] % 128 == 0
-        and grad_out.shape[1] % 512 == 0
+        and grad_out.shape[1] % (7 * 128) == 0
     )
     if suits:
-        return fused(4, *args)
+        return fused(7, *args)
     return plain(*args)
 
 

time: 98.5 us -> 93.9 us (0.953)
  Pallas kernels: 94.4 us -> 89.8 us
    pallas_call x1, Pallas kernels: 94.4 us -> 89.8 us  [fused(): pl.pallas_call(functools.partial(fused_kernel, chunks), out_shape=(jax.Sh...]
where the time goes in v3:
time: 93.9 us; the launch traced here: 93.7 us
  Pallas kernels  89.8 us (96%)
  local copies, waits for them, and re-layouts  3.25 us (3%)
    pallas_call x1, Pallas kernels, fused(): pl.pallas_call(functools.partial(fused_kernel, chunks), out_shape=(jax.Sh...  89.8 us
    unnamed x4, local copies, waits for them, and re-layouts  3.25 us

profile of v3, /device:TPU:0, one launch (start us, length us, event | category | flops | bytes accessed | tf_op | source)
XLA Modules:
  0.0 93.7 jit_solution(2494512610818920021)
XLA Ops:
  0.6 89.8 %shard_map.68 = (bf16[2,4,192,512]{3,2,1,0:T(8,128)(2,1)}, f32[8,128]{1,0:T(8,128)}) custom-call(bf16[128,3584]{1,0:T(8,128)(2,1)} %go_ref.1, bf16[8,128]{1,0:T(8,128)(2,1)} %bitcast.10, s32[4,128]{1,0:T(4,128)} %bitcast.11, bf16[1024,7168]{1,0:T(8,128)(2,1)} %bitcast.8, bf16[2,4,192,512]{3,2,1,0:T(8,128)(2,1)} %bitcast.9), custom_call_target="tpu_custom_call" | custom-call | flops 11274289152 | bytes 14680064 | tf_op jit(solution)/shard_map/pallas_call | solution.py:450
  90.4 0.0 copy-start
  90.4 2.7 %copy.9 = bf16[2,768,512]{2,1,0:T(8,128)(2,1)} copy(bf16[2,768,512]{2,1,0:T(8,128)(2,1)} %bitcast.6) | data formatting | bytes 3145728
  93.1 0.0 copy-done
  93.1 0.6 copy.10
Async XLA Ops:
  90.4 2.7 %copy-start = (f32[8,128]{1,0:T(8,128)S(1)}, f32[8,128]{1,0:T(8,128)}, u32[]{:S(2)}) copy-start(f32[8,128]{1,0:T(8,128)} %get-tuple-element.5) | copy-start | bytes 12292
